TPU v7x, 256 devices: a whole 4x4x8 slice. The times are simulated.
256 devices in a mesh: prow: 8 (over x, core), pcol: 32 (over z, y).
Axes of the slice: x: 4, y: 4, z: 8, core: 2. Of those that a mesh axis runs over, the one named last changes fastest.
Arguments:
- matrix: bfloat16 [4, 8, 512, 1, 32, 512], P(None, 'prow', None, None, 'pcol'), may hold values from -6 to 6
- upper_inv: bfloat16 [2, 512, 512], replicated, may hold values from -4 to 4
- lower_inv: bfloat16 [2, 512, 512], replicated, may hold values from -4 to 4
- solution: bfloat16 [1, 32, 512], P(None, 'pcol'), may hold values from -0.046875 to 0.046875
- right_side: float32 [4, 8, 512], P(None, 'prow'), may hold values from -6 to 6
- diagonal_block_inverses: bfloat16 [1, 8, 512, 512], P(None, 'prow'), may hold values from -0.009765625 to 0.009765625
Outputs:
- updated: bfloat16 [4, 8, 512, 1, 32, 512], P(None, 'prow', None, None, 'pcol')
- residual: float32 [4, 8, 512], P(None, 'prow')
- precond: float32 [8, 512], replicated
All inputs are finite; a program needn't handle non-finite values.
Results may differ from a plain program's by a relative error of at most 0.0085.
Values may be sent and summed in bfloat16 or wider, within the bound.
A program may use at most 128 MiB of HBM per device.

v0:
```python
import jax
import jax.numpy as jnp
from jax import lax
from jax.sharding import PartitionSpec as P

PANELS = 2


def broadcast(value, axis, source):
    kept = jnp.where(lax.axis_index(axis) == source, value, 0).astype(value.dtype)
    return lax.psum(kept, axis)


def shards(matrix, upper_inv, lower_inv, solution, right_side, diagonal_block_inverses):
    rows_blk = matrix.shape[0]
    cols_blk = matrix.shape[3]
    blk_width = matrix.shape[2]
    row_processors = lax.axis_size("prow")
    col_devs = lax.axis_size("pcol")
    col_index = lax.axis_index("pcol")
    base_matrix = matrix.reshape(rows_blk * blk_width, cols_blk * blk_width)
    current = base_matrix
    for section in range(PANELS):
        col_local = section // col_devs
        local_row_block = section // row_processors
        upper_tri = jnp.triu(upper_inv[section])
        lower_tri = jnp.tril(lower_inv[section])
        column = current
        row_band = current[local_row_block * blk_width : (local_row_block + 1) * blk_width, :]
        factored = jnp.dot(column, upper_tri, preferred_element_type=jnp.float32).astype(
            jnp.bfloat16
        )
        left_panel = broadcast(factored, "pcol", section % col_devs)
        top_local = jnp.dot(lower_tri, row_band, preferred_element_type=jnp.float32).astype(
            jnp.bfloat16
        )
        top_panel = broadcast(top_local, "prow", section % row_processors)
        current = (
            current.astype(jnp.float32)
            - jnp.dot(left_panel, top_panel, preferred_element_type=jnp.float32)
        ).astype(jnp.bfloat16)
    partial_value = jnp.dot(
        base_matrix, solution.reshape(cols_blk * blk_width), preferred_element_type=jnp.float32
    )
    totals = lax.psum(partial_value, "pcol")
    residual = right_side.reshape(rows_blk * blk_width) - totals
    res_blocks = residual.reshape(rows_blk, blk_width)
    slot_count = diagonal_block_inverses.shape[0]
    inverses = diagonal_block_inverses.reshape(slot_count, blk_width, blk_width)
    solve_count = slot_count * row_processors
    col_blocks = base_matrix.reshape(rows_blk * blk_width, cols_blk, blk_width)

    def carry_forward(blk_id, state):
        accum, solved = state
        owner_row = blk_id % row_processors
        slot_id = blk_id // row_processors
        pending = lax.dynamic_slice_in_dim(accum, slot_id * blk_width, blk_width, 0)
        res_block = lax.dynamic_slice_in_dim(res_blocks, slot_id, 1, 0)[0]
        inv_block = inverses[0].astype(jnp.float32)
        row_total = lax.psum(pending, "pcol")
        local_value = jnp.dot(inv_block, res_block - row_total, precision=lax.Precision.HIGHEST)
        new_value = broadcast(local_value, "prow", owner_row)
        rounded = new_value.astype(jnp.bfloat16)
        has_col = col_index == blk_id % col_devs
        col_piece = col_blocks[:, 0, :]
        product = jnp.dot(col_piece, rounded, preferred_element_type=jnp.float32)
        accum = accum + jnp.where(has_col, product, jnp.zeros_like(product))
        solved = lax.dynamic_update_slice_in_dim(solved, new_value[None], blk_id, 0)
        return (accum, solved)

    start = (
        jnp.zeros((rows_blk * blk_width,), jnp.float32),
        jnp.zeros((solve_count, blk_width), jnp.float32),
    )
    precond = lax.fori_loop(0, solve_count, carry_forward, start)[1]
    return (current.reshape(matrix.shape), residual.reshape(right_side.shape), precond)


def solution(mesh):
    return jax.shard_map(
        shards,
        mesh=mesh,
        in_specs=(
            P(None, "prow", None, None, "pcol", None),
            P(),
            P(),
            P(None, "pcol", None),
            P(None, "prow", None),
            P(None, "prow", None, None),
        ),
        out_specs=(P(None, "prow", None, None, "pcol", None), P(None, "prow", None), P()),
        check_vma=False,
    )
```

profile of v0, /device:TPU:1, one launch (start us, length us, event | category | flops | bytes accessed | tf_op | source)
XLA Modules:
  0.0 947.7 jit_solution(12790687416914332410)
XLA Ops:
  7.2 0.0 all-reduce.7.cloned.1.call-start
  7.3 2.6 fusion.5
  9.9 0.0 all-reduce.5.cloned.1.call-start
  10.0 2.9 fusion.3
  12.9 0.0 all-reduce.11.cloned.1.call-start
  12.9 0.6 fusion.32
  13.6 65.6 %psum.69 = f32[2048]{0:T(1024)S(1)} all-reduce(f32[2048]{0:T(1024)S(1)} %bitcast.79), channel_id=1, replica_groups=mesh['prow'=8,'pcol'=32] {'pcol'}, use_global_device_ids=true, to_apply=%region_4.5 | all-reduce | flops 2048 | bytes 16384 | tf_op jit(solution)/shard_map/psum | solution.py:45
  79.3 154.3 %all-reduce.5.cloned.1.call-done = bf16[2048,512]{0,1:T(8,128)(2,1)} async-done(((bf16[2048,512]{0,1:T(8,128)(2,1)}), bf16[2048,512]{0,1:T(8,128)(2,1)}) %all-reduce.5.cloned.1.call-update) | async-done | bytes 2097168 | tf_op jit(solution)/shard_map/psum | solution.py:11
  233.6 3.0 subtract_convert_fusion.1
  236.6 1.3 copy-done.7
  237.9 1.3 fusion.6
  239.2 0.0 all-reduce.9.cloned.1.call-start
  239.2 4.3 fusion.4
  243.6 1.0 copy-done.2
  244.6 691.6 %while.19 = (s32[]{:T(128)}, f32[2048]{0:T(1024)S(1)}, f32[8,512]{1,0:T(8,128)}, s32[]{:T(128)}, f32[4,512]{1,0:T(4,128)S(1)}, /*index=5*/bf16[1,1,512,512]{3,2,...) while((s32[]{:T(128)}, f32[2048]{0:T(1024)S(1)}, ...), condition=%wide.region_8.9_spmd.clone, body=%wide.region_5.8_spmd.clone.sunk | while | flops 5253665 | bytes 2712061 | solution.py:75
  244.6 0.1 dynamic_slice.28
  244.7 58.2 %psum.74 = f32[512]{0:T(512)S(1)} all-reduce(f32[512]{0:T(512)S(1)} %dynamic_slice.28), channel_id=1, replica_groups=mesh['prow'=8,'pcol'=32] {'pcol'}, use_global_device_ids=true, to_apply=%region_6.6 | all-reduce | flops 512 | bytes 4096 | tf_op jit(solution)/shard_map/while/body/eval_jaxpr/psum | solution.py:60
  302.9 0.5 fusion.59
  303.4 31.3 %psum.75 = f32[512]{0:T(512)S(1)} all-reduce(f32[512]{0:T(512)S(1)} %broadcast_select_fusion.5), channel_id=1, replica_groups=mesh['prow'=8,'pcol'=32] {'prow'}, use_global_device_ids=true, to_apply=%region_7.7 | all-reduce | flops 512 | bytes 4096 | tf_op jit(solution)/shard_map/while/body/eval_jaxpr/psum | solution.py:11
  334.7 0.6 fusion.60
  335.3 1.4 dynamic_update_slice.13
  336.7 0.1 dynamic_slice.28
  336.7 55.7 %psum.74 = f32[512]{0:T(512)S(1)} all-reduce(f32[512]{0:T(512)S(1)} %dynamic_slice.28), channel_id=1, replica_groups=mesh['prow'=8,'pcol'=32] {'pcol'}, use_global_device_ids=true, to_apply=%region_6.6 | all-reduce | flops 512 | bytes 4096 | tf_op jit(solution)/shard_map/while/body/eval_jaxpr/psum | solution.py:60
  392.5 0.5 fusion.59
  393.0 26.6 %psum.75 = f32[512]{0:T(512)S(1)} all-reduce(f32[512]{0:T(512)S(1)} %broadcast_select_fusion.5), channel_id=1, replica_groups=mesh['prow'=8,'pcol'=32] {'prow'}, use_global_device_ids=true, to_apply=%region_7.7 | all-reduce | flops 512 | bytes 4096 | tf_op jit(solution)/shard_map/while/body/eval_jaxpr/psum | solution.py:11
  419.6 0.6 fusion.60
  420.3 1.4 dynamic_update_slice.13
  421.6 0.1 dynamic_slice.28
  421.7 57.8 %psum.74 = f32[512]{0:T(512)S(1)} all-reduce(f32[512]{0:T(512)S(1)} %dynamic_slice.28), channel_id=1, replica_groups=mesh['prow'=8,'pcol'=32] {'pcol'}, use_global_device_ids=true, to_apply=%region_6.6 | all-reduce | flops 512 | bytes 4096 | tf_op jit(solution)/shard_map/while/body/eval_jaxpr/psum | solution.py:60
  479.5 0.5 fusion.59
  480.0 26.6 %psum.75 = f32[512]{0:T(512)S(1)} all-reduce(f32[512]{0:T(512)S(1)} %broadcast_select_fusion.5), channel_id=1, replica_groups=mesh['prow'=8,'pcol'=32] {'prow'}, use_global_device_ids=true, to_apply=%region_7.7 | all-reduce | flops 512 | bytes 4096 | tf_op jit(solution)/shard_map/while/body/eval_jaxpr/psum | solution.py:11
  506.7 0.6 fusion.60
  507.3 1.4 dynamic_update_slice.13
  508.7 0.1 dynamic_slice.28
  508.7 55.7 %psum.74 = f32[512]{0:T(512)S(1)} all-reduce(f32[512]{0:T(512)S(1)} %dynamic_slice.28), channel_id=1, replica_groups=mesh['prow'=8,'pcol'=32] {'pcol'}, use_global_device_ids=true, to_apply=%region_6.6 | all-reduce | flops 512 | bytes 4096 | tf_op jit(solution)/shard_map/while/body/eval_jaxpr/psum | solution.py:60
  564.5 0.5 fusion.59
  565.0 26.6 %psum.75 = f32[512]{0:T(512)S(1)} all-reduce(f32[512]{0:T(512)S(1)} %broadcast_select_fusion.5), channel_id=1, replica_groups=mesh['prow'=8,'pcol'=32] {'prow'}, use_global_device_ids=true, to_apply=%region_7.7 | all-reduce | flops 512 | bytes 4096 | tf_op jit(solution)/shard_map/while/body/eval_jaxpr/psum | solution.py:11
  591.5 0.6 fusion.60
  592.2 1.4 dynamic_update_slice.13
  593.6 0.1 dynamic_slice.28
  593.6 57.2 %psum.74 = f32[512]{0:T(512)S(1)} all-reduce(f32[512]{0:T(512)S(1)} %dynamic_slice.28), channel_id=1, replica_groups=mesh['prow'=8,'pcol'=32] {'pcol'}, use_global_device_ids=true, to_apply=%region_6.6 | all-reduce | flops 512 | bytes 4096 | tf_op jit(solution)/shard_map/while/body/eval_jaxpr/psum | solution.py:60
  650.8 0.5 fusion.59
  651.3 26.6 %psum.75 = f32[512]{0:T(512)S(1)} all-reduce(f32[512]{0:T(512)S(1)} %broadcast_select_fusion.5), channel_id=1, replica_groups=mesh['prow'=8,'pcol'=32] {'prow'}, use_global_device_ids=true, to_apply=%region_7.7 | all-reduce | flops 512 | bytes 4096 | tf_op jit(solution)/shard_map/while/body/eval_jaxpr/psum | solution.py:11
  678.0 0.6 fusion.60
  678.6 1.4 dynamic_update_slice.13
  680.0 0.1 dynamic_slice.28
  680.0 55.7 %psum.74 = f32[512]{0:T(512)S(1)} all-reduce(f32[512]{0:T(512)S(1)} %dynamic_slice.28), channel_id=1, replica_groups=mesh['prow'=8,'pcol'=32] {'pcol'}, use_global_device_ids=true, to_apply=%region_6.6 | all-reduce | flops 512 | bytes 4096 | tf_op jit(solution)/shard_map/while/body/eval_jaxpr/psum | solution.py:60
  735.8 0.5 fusion.59
  736.3 26.6 %psum.75 = f32[512]{0:T(512)S(1)} all-reduce(f32[512]{0:T(512)S(1)} %broadcast_select_fusion.5), channel_id=1, replica_groups=mesh['prow'=8,'pcol'=32] {'prow'}, use_global_device_ids=true, to_apply=%region_7.7 | all-reduce | flops 512 | bytes 4096 | tf_op jit(solution)/shard_map/while/body/eval_jaxpr/psum | solution.py:11
  762.9 0.6 fusion.60
  763.5 1.4 dynamic_update_slice.13
  764.9 0.1 dynamic_slice.28
  764.9 57.2 %psum.74 = f32[512]{0:T(512)S(1)} all-reduce(f32[512]{0:T(512)S(1)} %dynamic_slice.28), channel_id=1, replica_groups=mesh['prow'=8,'pcol'=32] {'pcol'}, use_global_device_ids=true, to_apply=%region_6.6 | all-reduce | flops 512 | bytes 4096 | tf_op jit(solution)/shard_map/while/body/eval_jaxpr/psum | solution.py:60
  822.1 0.5 fusion.59
  822.6 26.6 %psum.75 = f32[512]{0:T(512)S(1)} all-reduce(f32[512]{0:T(512)S(1)} %broadcast_select_fusion.5), channel_id=1, replica_groups=mesh['prow'=8,'pcol'=32] {'prow'}, use_global_device_ids=true, to_apply=%region_7.7 | all-reduce | flops 512 | bytes 4096 | tf_op jit(solution)/shard_map/while/body/eval_jaxpr/psum | solution.py:11
  849.3 0.6 fusion.60
  849.9 1.4 dynamic_update_slice.13
  851.3 0.1 dynamic_slice.28
  851.3 55.7 %psum.74 = f32[512]{0:T(512)S(1)} all-reduce(f32[512]{0:T(512)S(1)} %dynamic_slice.28), channel_id=1, replica_groups=mesh['prow'=8,'pcol'=32] {'pcol'}, use_global_device_ids=true, to_apply=%region_6.6 | all-reduce | flops 512 | bytes 4096 | tf_op jit(solution)/shard_map/while/body/eval_jaxpr/psum | solution.py:60
  907.1 0.5 fusion.59
  907.6 26.6 %psum.75 = f32[512]{0:T(512)S(1)} all-reduce(f32[512]{0:T(512)S(1)} %broadcast_select_fusion.5), channel_id=1, replica_groups=mesh['prow'=8,'pcol'=32] {'prow'}, use_global_device_ids=true, to_apply=%region_7.7 | all-reduce | flops 512 | bytes 4096 | tf_op jit(solution)/shard_map/while/body/eval_jaxpr/psum | solution.py:11
  934.2 0.6 fusion.60
  934.8 1.4 dynamic_update_slice.13
  936.2 5.0 subtract_convert_fusion
  (82 shorter events, 0.5 us)
Async XLA Ops:
  7.2 5.8 copy-start
  7.2 2.8 copy-start.1
  7.2 2.8 copy-start.6
  7.2 72.0 %all-reduce.7.cloned.1.call-start = ((), (), s32[]{:S(2)}) async-start(), calls=%async_computation.1 | async-start | bytes 1048576 | tf_op jit(solution)/shard_map/psum | solution.py:11
  9.9 223.7 %all-reduce.5.cloned.1.call-start = ((), (), s32[]{:S(2)}) async-start(), calls=%async_computation | async-start | bytes 4194304 | tf_op jit(solution)/shard_map/psum | solution.py:11
  12.8 66.3 %copy-start.4 = (f32[4,1,512]{2,1,0:T(1,128)S(1)}, f32[4,1,512]{2,1,0:T(1,128)}, u32[]{:S(2)}) copy-start(f32[4,1,512]{2,1,0:T(1,128)} %param.12) | copy-start | bytes 24580
  12.9 923.3 %all-reduce.11.cloned.1.call-start = ((), (), s32[]{:S(2)}) async-start(), calls=%async_computation.3 | async-start | bytes 1048576 | tf_op jit(solution)/shard_map/psum | solution.py:11
  79.2 157.4 %copy-start.3 = (f32[2048]{0:T(1024)}, f32[2048]{0:T(1024)S(1)}, u32[]{:S(2)}) copy-start(f32[2048]{0:T(1024)S(1)} %sub.28) | copy-start | bytes 24580
  79.2 158.7 %copy-start.5 = (bf16[2,512,512]{2,1,0:T(8,128)(2,1)S(1)}, bf16[2,512,512]{2,1,0:T(8,128)(2,1)}, u32[]{:S(2)}) copy-start(bf16[2,512,512]{2,1,0:T(8,128)(2,1)} %param.10) | copy-start | bytes 3145732
  236.6 1.3 copy-start.7
  239.2 697.0 %all-reduce.9.cloned.1.call-start = ((), (), s32[]{:S(2)}) async-start(), calls=%async_computation.2 | async-start | bytes 4194304 | tf_op jit(solution)/shard_map/psum | solution.py:11
  243.6 1.0 copy-start.2
Sparse Core Ops, SparseCore 0:
  10.4 67.5 all-reduce.6
  82.5 151.0 all-reduce.4
  239.3 64.9 all-reduce.10
  308.1 151.9 all-reduce.8
where the time goes:
time: 949 us; the launch traced here: 948 us
  blocking collectives  736 us (78%)
  waiting for transfers between devices  154 us (16%)
  matrix products  28.7 us (3%)
  local copies, waits for them, and re-layouts  13.9 us (1%)
  between operations  13.9 us (1%)
    psum x8, blocking collectives, carry_forward(): row_total = lax.psum(pending, 'pcol')  453 us
    psum x8, blocking collectives, broadcast(): return lax.psum(kept, axis)  217 us
    psum x4, waiting for transfers between devices, broadcast(): return lax.psum(kept, axis)  154 us
    psum x1, blocking collectives, shards(): totals = lax.psum(partial_value, 'pcol')  65.6 us
  transfers between devices with their start and end apart: 4, of which 1 were waited for; matrix products, arithmetic and copies ran while one was open for 3% of the time, Pallas kernels for 0%

commit v1 on v0

--- a/solution.py
+++ b/solution.py
@@ -4,6 +4,15 @@
 from jax.sharding import PartitionSpec as P
 
 PANELS = 2
+
+
+def doubling_sum(x, name):
+    n_dev = lax.axis_size(name)
+    acc, far = (x, 1)
+    while far < n_dev:
+        acc = acc + lax.ppermute(acc, name, [(i, i ^ far) for i in range(n_dev)])
+        far = 2 * far
+    return acc
 
 
 def broadcast(value, axis, source):
@@ -57,7 +66,7 @@
         pending = lax.dynamic_slice_in_dim(accum, slot_id * blk_width, blk_width, 0)
         res_block = lax.dynamic_slice_in_dim(res_blocks, slot_id, 1, 0)[0]
         inv_block = inverses[0].astype(jnp.float32)
-        row_total = lax.psum(pending, "pcol")
+        row_total = doubling_sum(pending, "pcol")
         local_value = jnp.dot(inv_block, res_block - row_total, precision=lax.Precision.HIGHEST)
         new_value = broadcast(local_value, "prow", owner_row)
         rounded = new_value.astype(jnp.bfloat16)

time: 949 us -> 792 us (0.83)
  blocking collectives: 736 us -> 208 us
  waiting for transfers between devices: 154 us -> 482 us
  starting transfers between devices: 0.16 us -> 43.1 us
    psum x8 -> x0, blocking collectives: 453 us -> none  [carry_forward(): row_total = lax.psum(pending, 'pcol')]
    psum x4, waiting for transfers between devices: 154 us -> 376 us  [broadcast(): return lax.psum(kept, axis)]
    ppermute x0 -> x40, waiting for transfers between devices: none -> 106 us  [doubling_sum(): acc = acc + lax.ppermute(acc, name, [(i, i ^ far) for i in range(n_dev)])]
    psum x8, blocking collectives: 217 us -> 149 us  [broadcast(): return lax.psum(kept, axis)]
    ppermute x0 -> x40, starting transfers between devices: none -> 43 us  [doubling_sum(): acc = acc + lax.ppermute(acc, name, [(i, i ^ far) for i in range(n_dev)])]
  transfers between devices with their start and end apart: 4 -> 44, of which waited for: 1 -> 44; matrix products, arithmetic and copies ran while one was open for 3% -> 1% of each run, Pallas kernels for 0% -> 0%
where the time goes in v1:
time: 792 us; the launch traced here: 790 us
  waiting for transfers between devices  482 us (61%)
  blocking collectives  208 us (26%)
  starting transfers between devices  43.1 us (5%)
  matrix products  28.7 us (4%)
  between operations  13.9 us (2%)
  local copies, waits for them, and re-layouts  12.9 us (2%)
    psum x4, waiting for transfers between devices, broadcast(): return lax.psum(kept, axis)  376 us
    psum x8, blocking collectives, broadcast(): return lax.psum(kept, axis)  149 us
    ppermute x40, waiting for transfers between devices, doubling_sum(): acc = acc + lax.ppermute(acc, name, [(i, i ^ far) for i in range(n_dev)])  106 us
    psum x1, blocking collectives, shards(): totals = lax.psum(partial_value, 'pcol')  59.2 us
    ppermute x40, starting transfers between devices, doubling_sum(): acc = acc + lax.ppermute(acc, name, [(i, i ^ far) for i in range(n_dev)])  43 us
  transfers between devices with their start and end apart: 44, of which 44 were waited for; matrix products, arithmetic and copies ran while one was open for 1% of the time, Pallas kernels for 0%

profile of v1, /device:TPU:1, one launch (start us, length us, event | category | flops | bytes accessed | tf_op | source)
XLA Modules:
  0.0 790.5 jit_solution(3818912720331743034)
XLA Ops:
  7.3 2.6 fusion.5
  10.0 2.9 fusion.3
  12.9 65.0 %all-reduce.7.cloned.1.call-done = bf16[512,512]{1,0:T(8,128)(2,1)} async-done(((bf16[512,512]{1,0:T(8,128)(2,1)}), bf16[512,512]{1,0:T(8,128)(2,1)}) %all-reduce.7.cloned.1.call-update) | async-done | bytes 524304 | tf_op jit(solution)/shard_map/psum | solution.py:20
  77.9 155.7 %all-reduce.5.cloned.1.call-done = bf16[2048,512]{0,1:T(8,128)(2,1)} async-done(((bf16[2048,512]{0,1:T(8,128)(2,1)}), bf16[2048,512]{0,1:T(8,128)(2,1)}) %all-reduce.5.cloned.1.call-update) | async-done | bytes 2097168 | tf_op jit(solution)/shard_map/psum | solution.py:20
  233.6 3.0 subtract_convert_fusion.1
  239.2 4.3 fusion.4
  244.2 59.2 %psum.54 = f32[2048]{0:T(1024)S(1)} all-reduce(f32[2048]{0:T(1024)S(1)} %bitcast.79), channel_id=1, replica_groups=mesh['prow'=8,'pcol'=32] {'pcol'}, use_global_device_ids=true, to_apply=%region_4.5 | all-reduce | flops 2048 | bytes 16384 | tf_op jit(solution)/shard_map/psum | solution.py:54
  304.3 154.9 %all-reduce.9.cloned.1.call-done = bf16[2048,512]{1,0:T(8,128)(2,1)} async-done(((bf16[2048,512]{1,0:T(8,128)(2,1)}), bf16[2048,512]{1,0:T(8,128)(2,1)}) %all-reduce.9.cloned.1.call-update) | async-done | bytes 2097168 | tf_op jit(solution)/shard_map/psum | solution.py:20
  459.2 5.0 subtract_convert_fusion
  464.2 319.7 %while.19 = (s32[]{:T(128)}, f32[2048]{0:T(1024)S(1)}, f32[8,512]{1,0:T(8,128)}, s32[]{:T(128)}, f32[4,512]{1,0:T(4,128)S(1)}, /*index=5*/bf16[1,1,512,512]{3,2,...) while((s32[]{:T(128)}, f32[2048]{0:T(1024)S(1)}, ...), condition=%wide.region_7.8_spmd.clone, body=%wide.region_5.7_spmd.clone.sunk | while | flops 5255713 | bytes 2775761 | solution.py:84
  468.4 2.4 collective-permute-done.1
  471.0 2.2 collective-permute-done.2
  476.6 3.3 collective-permute-start.4
  479.9 3.0 collective-permute-done.4
  483.4 22.7 %psum.57 = f32[512]{0:T(512)S(1)} all-reduce(f32[512]{0:T(512)S(1)} %broadcast_select_fusion.5), channel_id=1, replica_groups=mesh['prow'=8,'pcol'=32] {'prow'}, use_global_device_ids=true, to_apply=%region_6.6 | all-reduce | flops 512 | bytes 4096 | tf_op jit(solution)/shard_map/while/body/eval_jaxpr/psum | solution.py:20
  508.3 2.4 collective-permute-done
  511.9 2.8 collective-permute-done.1
  514.9 2.4 collective-permute-done.2
  518.4 2.2 collective-permute-done.3
  520.6 2.6 collective-permute-start.4
  523.2 3.7 collective-permute-done.4
  527.5 18.1 %psum.57 = f32[512]{0:T(512)S(1)} all-reduce(f32[512]{0:T(512)S(1)} %broadcast_select_fusion.5), channel_id=1, replica_groups=mesh['prow'=8,'pcol'=32] {'prow'}, use_global_device_ids=true, to_apply=%region_6.6 | all-reduce | flops 512 | bytes 4096 | tf_op jit(solution)/shard_map/while/body/eval_jaxpr/psum | solution.py:20
  547.7 2.4 collective-permute-done
  551.3 2.8 collective-permute-done.1
  554.3 2.4 collective-permute-done.2
  557.8 2.2 collective-permute-done.3
  560.0 2.6 collective-permute-start.4
  562.6 3.7 collective-permute-done.4
  566.9 18.1 %psum.57 = f32[512]{0:T(512)S(1)} all-reduce(f32[512]{0:T(512)S(1)} %broadcast_select_fusion.5), channel_id=1, replica_groups=mesh['prow'=8,'pcol'=32] {'prow'}, use_global_device_ids=true, to_apply=%region_6.6 | all-reduce | flops 512 | bytes 4096 | tf_op jit(solution)/shard_map/while/body/eval_jaxpr/psum | solution.py:20
  587.1 2.4 collective-permute-done
  590.7 2.8 collective-permute-done.1
  593.7 2.4 collective-permute-done.2
  597.2 2.2 collective-permute-done.3
  599.4 2.6 collective-permute-start.4
  602.0 3.7 collective-permute-done.4
  606.3 18.1 %psum.57 = f32[512]{0:T(512)S(1)} all-reduce(f32[512]{0:T(512)S(1)} %broadcast_select_fusion.5), channel_id=1, replica_groups=mesh['prow'=8,'pcol'=32] {'prow'}, use_global_device_ids=true, to_apply=%region_6.6 | all-reduce | flops 512 | bytes 4096 | tf_op jit(solution)/shard_map/while/body/eval_jaxpr/psum | solution.py:20
  626.5 2.4 collective-permute-done
  630.1 2.8 collective-permute-done.1
  633.1 2.4 collective-permute-done.2
  636.6 2.2 collective-permute-done.3
  638.8 2.6 collective-permute-start.4
  641.4 3.7 collective-permute-done.4
  645.7 18.1 %psum.57 = f32[512]{0:T(512)S(1)} all-reduce(f32[512]{0:T(512)S(1)} %broadcast_select_fusion.5), channel_id=1, replica_groups=mesh['prow'=8,'pcol'=32] {'prow'}, use_global_device_ids=true, to_apply=%region_6.6 | all-reduce | flops 512 | bytes 4096 | tf_op jit(solution)/shard_map/while/body/eval_jaxpr/psum | solution.py:20
  665.9 2.4 collective-permute-done
  669.5 2.8 collective-permute-done.1
  672.5 2.4 collective-permute-done.2
  676.0 2.2 collective-permute-done.3
  678.2 2.6 collective-permute-start.4
  680.8 3.7 collective-permute-done.4
  685.1 18.1 %psum.57 = f32[512]{0:T(512)S(1)} all-reduce(f32[512]{0:T(512)S(1)} %broadcast_select_fusion.5), channel_id=1, replica_groups=mesh['prow'=8,'pcol'=32] {'prow'}, use_global_device_ids=true, to_apply=%region_6.6 | all-reduce | flops 512 | bytes 4096 | tf_op jit(solution)/shard_map/while/body/eval_jaxpr/psum | solution.py:20
  705.3 2.4 collective-permute-done
  708.9 2.8 collective-permute-done.1
  711.9 2.4 collective-permute-done.2
  715.4 2.2 collective-permute-done.3
  717.6 2.6 collective-permute-start.4
  720.3 3.7 collective-permute-done.4
  724.5 18.1 %psum.57 = f32[512]{0:T(512)S(1)} all-reduce(f32[512]{0:T(512)S(1)} %broadcast_select_fusion.5), channel_id=1, replica_groups=mesh['prow'=8,'pcol'=32] {'prow'}, use_global_device_ids=true, to_apply=%region_6.6 | all-reduce | flops 512 | bytes 4096 | tf_op jit(solution)/shard_map/while/body/eval_jaxpr/psum | solution.py:20
  744.7 2.4 collective-permute-done
  748.3 2.8 collective-permute-done.1
  751.3 2.4 collective-permute-done.2
  754.8 2.2 collective-permute-done.3
  757.0 2.6 collective-permute-start.4
  759.7 3.7 collective-permute-done.4
  763.9 18.1 %psum.57 = f32[512]{0:T(512)S(1)} all-reduce(f32[512]{0:T(512)S(1)} %broadcast_select_fusion.5), channel_id=1, replica_groups=mesh['prow'=8,'pcol'=32] {'prow'}, use_global_device_ids=true, to_apply=%region_6.6 | all-reduce | flops 512 | bytes 4096 | tf_op jit(solution)/shard_map/while/body/eval_jaxpr/psum | solution.py:20
  (186 shorter events, 50.8 us)
Async XLA Ops:
  7.2 236.4 %copy-start = (bf16[1,1,512]{2,1,0:T(2,128)(2,1)S(1)}, bf16[1,1,512]{2,1,0:T(2,128)(2,1)}, u32[]{:S(2)}) copy-start(bf16[1,1,512]{2,1,0:T(2,128)(2,1)} %param.11) | copy-start | bytes 3076
  7.2 2.8 copy-start.1
  7.2 2.8 copy-start.6
  7.2 70.7 %all-reduce.7.cloned.1.call-start = ((), (), s32[]{:S(2)}) async-start(), calls=%async_computation.1 | async-start | bytes 1048576 | tf_op jit(solution)/shard_map/psum | solution.py:20
  9.9 223.7 %all-reduce.5.cloned.1.call-start = ((), (), s32[]{:S(2)}) async-start(), calls=%async_computation | async-start | bytes 4194304 | tf_op jit(solution)/shard_map/psum | solution.py:20
  12.9 291.5 %all-reduce.11.cloned.1.call-start = ((), (), s32[]{:S(2)}) async-start(), calls=%async_computation.3 | async-start | bytes 1048576 | tf_op jit(solution)/shard_map/psum | solution.py:20
  12.9 225.0 %copy-start.5 = (bf16[2,512,512]{2,1,0:T(8,128)(2,1)S(1)}, bf16[2,512,512]{2,1,0:T(8,128)(2,1)}, u32[]{:S(2)}) copy-start(bf16[2,512,512]{2,1,0:T(8,128)(2,1)} %param.10) | copy-start | bytes 3145732
  236.6 1.3 copy-start.7
  239.2 220.1 %all-reduce.9.cloned.1.call-start = ((), (), s32[]{:S(2)}) async-start(), calls=%async_computation.2 | async-start | bytes 4194304 | tf_op jit(solution)/shard_map/psum | solution.py:20
  243.5 59.9 %copy-start.4 = (f32[4,1,512]{2,1,0:T(1,128)S(1)}, f32[4,1,512]{2,1,0:T(1,128)}, u32[]{:S(2)}) copy-start(f32[4,1,512]{2,1,0:T(1,128)} %param.12) | copy-start | bytes 24580
  303.4 160.8 %copy-start.3 = (f32[2048]{0:T(1024)}, f32[2048]{0:T(1024)S(1)}, u32[]{:S(2)}) copy-start(f32[2048]{0:T(1024)S(1)} %sub.28) | copy-start | bytes 24580
  303.5 160.8 %copy-start.2 = (bf16[1,1,512,512]{3,2,1,0:T(8,128)(2,1)S(1)}, bf16[1,1,512,512]{3,2,1,0:T(8,128)(2,1)}, u32[]{:S(2)}) copy-start(bf16[1,1,512,512]{3,2,1,0:T(8,128)(2,1)} %param.13) | copy-start | bytes 1572868
  464.3 2.5 collective-permute-start
  466.8 4.0 collective-permute-start.1
  470.8 2.4 collective-permute-start.2
  473.3 3.3 collective-permute-start.3
  476.6 6.3 collective-permute-start.4
  508.2 2.5 collective-permute-start
  510.8 4.0 collective-permute-start.1
  514.7 2.5 collective-permute-start.2
  517.3 3.3 collective-permute-start.3
  520.6 6.3 collective-permute-start.4
  547.6 2.5 collective-permute-start
  550.2 4.0 collective-permute-start.1
  554.1 2.5 collective-permute-start.2
  556.7 3.3 collective-permute-start.3
  560.0 6.3 collective-permute-start.4
  587.0 2.5 collective-permute-start
  589.6 4.0 collective-permute-start.1
  593.5 2.5 collective-permute-start.2
  596.1 3.3 collective-permute-start.3
  599.4 6.3 collective-permute-start.4
  626.4 2.5 collective-permute-start
  629.0 4.0 collective-permute-start.1
  632.9 2.5 collective-permute-start.2
  635.5 3.3 collective-permute-start.3
  638.8 6.3 collective-permute-start.4
  665.8 2.5 collective-permute-start
  668.4 4.0 collective-permute-start.1
  672.3 2.5 collective-permute-start.2
  674.9 3.3 collective-permute-start.3
  678.2 6.3 collective-permute-start.4
  705.2 2.5 collective-permute-start
  707.8 4.0 collective-permute-start.1
  711.7 2.5 collective-permute-start.2
  714.3 3.3 collective-permute-start.3
  717.6 6.3 collective-permute-start.4
  744.6 2.5 collective-permute-start
  747.2 4.0 collective-permute-start.1
  751.1 2.5 collective-permute-start.2
  753.7 3.3 collective-permute-start.3
  757.0 6.3 collective-permute-start.4
Sparse Core Ops, SparseCore 0:
  10.4 67.4 all-reduce.6
  82.4 151.1 all-reduce.4
  239.3 64.9 all-reduce.10
  308.1 151.0 all-reduce.8
